TPU v7x, 512 devices: a whole 4x4x16 slice. The times are simulated.
512 devices in a mesh: tp: 8 (over y, core), ad: 64 (over z, x).
Axes of the slice: x: 4, y: 4, z: 16, core: 2. Of those that a mesh axis runs over, the one named last changes fastest.
Arguments:
- tokens: bfloat16 [16384, 4096], P('ad', 'tp'), may hold values from -6 to 6
- key_value_weight: bfloat16 [4096, 2048], P('tp'), may hold values from -0.09375 to 0.09375
- adapter_down_weight: bfloat16 [512, 32, 4096], P('ad', None, 'tp'), may hold values from -0.09375 to 0.09375
- adapter_up_weight: bfloat16 [512, 16, 2048], P('ad', None, 'tp'), may hold values from -1.5 to 1.5
- request_adapter_index: int32 [4096], P('ad'), may hold values from 0 to 511, as said below
- lengths: int32 [64, 64], P('ad'), may hold values from 1 to 8, 256 in all within a row
Outputs:
- mixed: bfloat16 [16384, 2048], P('ad', 'tp')
Inputs may be any that keep to these rules, and one draw needn't show every extreme that they name: `request_adapter_index`: owner o stores adapters o * 8 to (o+1) * 8 - 1. Among the 64 requests of one token group, the adapters of exactly one owner are named by exactly 2 requests and those of every other owner by at most one.
All inputs are finite; a program needn't handle non-finite values.
Results may differ from a plain program's by a relative error of at most 0.018.
Values may be sent and summed in bfloat16 or wider, within the bound.
No kernel may reach another device: no remote copies, remote signals or barrier semaphores. Data moves between devices by JAX's collectives and lax.ppermute only.
A program may use at most 64 MiB of HBM per device.

v0:
```python
import jax
import jax.numpy as jnp
from jax import lax
from jax.sharding import PartitionSpec as P

OWNER_SLOTS = 2
ADAPTER_SCALE = 2.0


def local(
    tokens, key_value_weight, adapter_down_weight, adapter_up_weight, request_adapter_index, lengths
):
    tok_rows, width = tokens.shape
    n_ad = lax.axis_size("ad")
    n_tp = lax.axis_size("tp")
    stored_factors = adapter_down_weight.shape[0]
    doubled_rank = adapter_down_weight.shape[1]
    rank_rows = adapter_up_weight.shape[1]
    column_range = adapter_up_weight.shape[2]
    half_cols = column_range * n_tp // 2
    requests = request_adapter_index.shape[0]
    slots = n_ad * OWNER_SLOTS
    longest = 2 * tok_rows // n_ad
    lens = lengths[0]
    ends = jnp.cumsum(lens)
    starts = ends - lens
    owner = request_adapter_index // stored_factors
    inside = request_adapter_index % stored_factors
    order = jnp.arange(requests, dtype=jnp.int32)
    earlier = (owner[:, None] == owner[None, :]) & (order[None, :] < order[:, None])
    slot_of = owner * OWNER_SLOTS + jnp.sum(earlier.astype(jnp.int32), axis=1)
    hits = slot_of[None, :] == jnp.arange(slots, dtype=jnp.int32)[:, None]
    slot_used = jnp.any(hits, axis=1)
    slot_req = jnp.sum(jnp.where(hits, order[None, :], 0), axis=1)
    slot_ids = jnp.sum(jnp.where(hits, inside[None, :], 0), axis=1)
    offsets = jnp.arange(longest, dtype=jnp.int32)
    live = slot_used[:, None] & (offsets[None, :] < lens[slot_req][:, None])
    take = jnp.where(live, starts[slot_req][:, None] + offsets[None, :], 0)
    slot_rows = jnp.where(live[:, :, None], tokens[take], jnp.zeros((), tokens.dtype))
    positions = jnp.arange(tok_rows, dtype=jnp.int32)
    request_of = jnp.sum((positions[:, None] >= ends[None, :]).astype(jnp.int32), axis=1)
    back = slot_of[request_of] * longest + positions - starts[request_of]
    wanted_rows = lax.all_to_all(
        slot_ids.reshape(n_ad, OWNER_SLOTS), "ad", split_axis=0, concat_axis=0, tiled=True
    )
    selected_up_factor = adapter_up_weight[wanted_rows]
    down_got, up_got = (
        lax.all_to_all(
            adapter_down_weight[wanted_rows], "ad", split_axis=0, concat_axis=0, tiled=True
        ),
        lax.all_to_all(selected_up_factor, "ad", split_axis=0, concat_axis=0, tiled=True),
    )
    low_slots = jnp.einsum(
        "smd,scd->smc",
        slot_rows,
        down_got.reshape(slots, doubled_rank, width),
        preferred_element_type=jnp.float32,
    )
    partial_value = jnp.dot(tokens, key_value_weight, preferred_element_type=jnp.float32)
    base_output = lax.psum_scatter(
        partial_value.astype(jnp.bfloat16), "tp", scatter_dimension=1, tiled=True
    ).astype(jnp.float32)
    low_tokens = low_slots.reshape(slots * longest, doubled_rank)[back]
    low = lax.psum(low_tokens.astype(jnp.bfloat16), "tp").astype(jnp.float32)
    half = lax.axis_index("tp") * column_range // half_cols
    low_half = lax.dynamic_slice_in_dim(low, half * rank_rows, rank_rows, 1)
    low_padded = jnp.where(live[:, :, None], low_half[take], jnp.float32(0.0))
    up_float = up_got.reshape(slots, rank_rows, column_range).astype(jnp.float32)
    delta_slots = jnp.einsum("smc,sck->smk", low_padded, up_float, precision=lax.Precision.HIGHEST)
    adapter_delta = delta_slots.reshape(slots * longest, column_range)[back]
    return (base_output + ADAPTER_SCALE * adapter_delta).astype(jnp.bfloat16)


def solution(mesh):
    return jax.shard_map(
        local,
        mesh=mesh,
        in_specs=(
            P("ad", "tp"),
            P("tp", None),
            P("ad", None, "tp"),
            P("ad", None, "tp"),
            P("ad"),
            P("ad", None),
        ),
        out_specs=P("ad", "tp"),
        check_vma=False,
    )
```

profile of v0, /device:TPU:8, one launch (start us, length us, event | category | flops | bytes accessed | tf_op | source)
XLA Modules:
  0.0 312.2 jit_solution(7859275561999897293)
XLA Ops:
  6.5 0.8 and_select_fusion
  7.4 0.2 convert_reduce_fusion.1
  7.8 33.0 %all_to_all.22 = s32[64,1,2]{2,1,0:T(1,128)S(1)} all-to-all(s32[64,1,2]{2,1,0:T(1,128)S(1)} %bitcast.41), channel_id=1, replica_groups=mesh['tp'=8,'ad'=64] {'ad'}, dimensions={0} | all-to-all | bytes 1024 | tf_op jit(solution)/shard_map/all_to_all | solution.py:43
  40.9 0.1 reshape.291
  41.1 3.7 %gather_fusion.3 = bf16[128,32,512]{2,1,0:T(8,128)(2,1)} fusion(bf16[8,32,512]{2,1,0:T(8,128)(2,1)} %param.8, s32[1024]{0:T(1024)S(1)} %pad_clamp_fusion.2), kind=kCustom, calls=%fused_computation.3 | custom fusion | bytes 8389120 | tf_op jit(solution)/shard_map/gather | solution.py:49
  44.8 5.8 %all-to-all-start.1 = ((bf16[64,2,32,512]{3,2,1,0:T(8,128)(2,1)}), bf16[64,2,32,512]{3,2,1,0:T(8,128)(2,1)}, u32[]{:S(2)}, u32[]{:S(2)}) async-start(bf16[64,2,32,512]{3,2,1,0:T(8,128)(2,1)} %bitcast.39), calls=%async_computation.2 | async-start | bytes 8388608 | tf_op jit(solution)/shard_map/all_to_all | solution.py:48
  50.7 1.7 gather_fusion.8
  52.4 187.1 %all-to-all-done.1 = bf16[64,2,32,512]{3,2,1,0:T(8,128)(2,1)} async-done(((bf16[64,2,32,512]{3,2,1,0:T(8,128)(2,1)}), bf16[64,2,32,512]{3,2,1,0:T(8,128)(2,1)}, u32[]{:S(2)}, u32[]{:S(2)}) %all-to-all-start.1) | async-done | bytes 4194336 | tf_op jit(solution)/shard_map/all_to_all | solution.py:48
  239.4 5.8 %all-to-all-start.2 = ((bf16[64,2,16,256]{3,2,1,0:T(8,128)(2,1)}), bf16[64,2,16,256]{3,2,1,0:T(8,128)(2,1)S(1)}, u32[]{:S(2)}, u32[]{:S(2)}) async-start(bf16[64,2,16,256]{3,2,1,0:T(8,128)(2,1)} %bitcast.16), calls=%async_computation.3 | async-start | bytes 2097152 | tf_op jit(solution)/shard_map/all_to_all | solution.py:51
  245.4 1.7 convolution_convert_fusion
  247.6 1.9 gather_fusion.4
  249.5 1.9 gather_fusion.5
  251.3 1.2 gather_fusion.1
  252.6 1.2 gather_fusion
  254.1 5.1 %gather_fusion.2 = bf16[1024,512]{1,0:T(8,128)(2,1)} fusion(bf16[256,512]{1,0:T(8,128)(2,1)S(1)} %copy-done.2, s32[1024]{0:T(1024)S(1)} %broadcast_clamp_fusion), kind=kCustom, calls=%fused_computation.2 | custom fusion | bytes 2101248 | tf_op jit(solution)/shard_map/gather | solution.py:39
  259.3 3.8 %convolution_bitcast_fusion.1 = bf16[1024,32]{1,0:T(8,128)(2,1)S(1)} fusion(bf16[128,32,512]{2,1,0:T(8,128)(2,1)} %bitcast.8, bf16[1024,512]{1,0:T(8,128)(2,1)} %gather_fusion.2, pred[128,8]{1,0:T(8,128)(4,1)S(1)} %fusion.4), kind=kOutput, calls=%fused_computation.12 | convolution fusion | flops 34078720 | bytes 5309440 | tf_op jit(solution)/shard_map/smd,scd->smc/dot_general | solution.py:53
  263.1 0.9 gather_fusion.6
  264.0 23.1 %psum.7 = bf16[256,32]{1,0:T(8,128)(2,1)S(1)} all-reduce(bf16[256,32]{1,0:T(8,128)(2,1)S(1)} %gather_fusion.6), channel_id=1, replica_groups=mesh['tp'=8,'ad'=64] {'tp'}, use_global_device_ids=true, to_apply=%region_7.8 | all-reduce | flops 8192 | bytes 32768 | tf_op jit(solution)/shard_map/psum | solution.py:64
  287.2 4.0 %gather_fusion.7 = f32[1024,16]{1,0:T(8,128)} fusion(f32[256,16]{1,0:T(8,128)S(1)} %dynamic-slice_convert_fusion, s32[1024]{0:T(1024)S(1)} %broadcast_clamp_fusion), kind=kCustom, calls=%fused_computation.7 | custom fusion | bytes 135168 | tf_op jit(solution)/shard_map/gather | solution.py:67
  291.2 8.6 %all-to-all-done.2 = bf16[64,2,16,256]{3,2,1,0:T(8,128)(2,1)S(1)} async-done(((bf16[64,2,16,256]{3,2,1,0:T(8,128)(2,1)}), bf16[64,2,16,256]{3,2,1,0:T(8,128)(2,1)S(1)}, u32[]{:S(2)}, u32[]{:S(2)}) %all-to-all-start.2) | async-done | bytes 1048608 | tf_op jit(solution)/shard_map/all_to_all | solution.py:51
  299.8 1.0 copy-done.4
  300.8 2.0 convolution_bitcast_fusion
  302.8 1.0 gather_fusion.9
  303.8 1.6 add_convert_fusion
  (37 shorter events, 1.5 us)
Async XLA Ops:
  6.5 238.8 %copy-start = (bf16[512,2048]{1,0:T(8,128)(2,1)S(1)}, bf16[512,2048]{1,0:T(8,128)(2,1)}, u32[]{:S(2)}) copy-start(bf16[512,2048]{1,0:T(8,128)(2,1)} %param.7) | copy-start | bytes 6291460
  44.8 5.8 %copy-start.3 = (bf16[8,16,256]{2,1,0:T(8,128)(2,1)S(1)}, bf16[8,16,256]{2,1,0:T(8,128)(2,1)}, u32[]{:S(2)}) copy-start(bf16[8,16,256]{2,1,0:T(8,128)(2,1)} %param.9) | copy-start | bytes 196612
  44.8 194.6 %all-to-all-start.1 = ((bf16[64,2,32,512]{3,2,1,0:T(8,128)(2,1)}), bf16[64,2,32,512]{3,2,1,0:T(8,128)(2,1)}, u32[]{:S(2)}, u32[]{:S(2)}) async-start(bf16[64,2,32,512]{3,2,1,0:T(8,128)(2,1)} %bitcast.39), calls=%async_computation.2 | async-start | bytes 8388608 | tf_op jit(solution)/shard_map/all_to_all | solution.py:48
  50.6 194.7 %copy-start.2 = (bf16[256,512]{1,0:T(8,128)(2,1)S(1)}, bf16[256,512]{1,0:T(8,128)(2,1)}, u32[]{:S(2)}) copy-start(bf16[256,512]{1,0:T(8,128)(2,1)} %param.6) | copy-start | bytes 786436
  50.7 196.5 %copy-start.1 = (s32[1,64]{1,0:T(1,128)S(1)}, s32[1,64]{1,0:T(1,128)}, u32[]{:S(2)}) copy-start(s32[1,64]{1,0:T(1,128)} %param.11) | copy-start | bytes 772
  239.4 60.3 %all-to-all-start.2 = ((bf16[64,2,16,256]{3,2,1,0:T(8,128)(2,1)}), bf16[64,2,16,256]{3,2,1,0:T(8,128)(2,1)S(1)}, u32[]{:S(2)}, u32[]{:S(2)}) async-start(bf16[64,2,16,256]{3,2,1,0:T(8,128)(2,1)} %bitcast.16), calls=%async_computation.3 | async-start | bytes 2097152 | tf_op jit(solution)/shard_map/all_to_all | solution.py:51
  245.3 58.5 %reduce-scatter.2.cloned.1.call-start = ((), (), s32[]{:S(2)}) async-start(), calls=%async_computation.4 | async-start | bytes 1179648 | tf_op jit(solution)/shard_map/reduce_scatter | solution.py:60
  299.8 1.0 copy-start.4
Sparse Core Ops, SparseCore 0:
  249.0 37.8 reduce-scatter.1
where the time goes:
time: 313 us; the launch traced here: 312 us
  waiting for transfers between devices  196 us (63%)
  blocking collectives  56.1 us (18%)
  local copies, waits for them, and re-layouts  24.2 us (8%)
  between operations  13.6 us (4%)
  starting transfers between devices  11.7 us (4%)
  matrix products  7.52 us (2%)
  other arithmetic  3.46 us (1%)
    all_to_all x1, waiting for transfers between devices, local(): lax.all_to_all(adapter_down_weight[wanted_rows], 'ad', split_axis=0, conc...  187 us
    all_to_all x1, blocking collectives, local(): lax.all_to_all(slot_ids.reshape(n_ad, OWNER_SLOTS), 'ad', split_axis=0, c...  33 us
    psum x1, blocking collectives, local(): low = lax.psum(low_tokens.astype(jnp.bfloat16), 'tp').astype(jnp.float32)  23.1 us
    all_to_all x1, waiting for transfers between devices, local(): lax.all_to_all(selected_up_factor, 'ad', split_axis=0, concat_axis=0, til...  8.62 us
  transfers between devices with their start and end apart: 3, of which 2 were waited for; matrix products, arithmetic and copies ran while one was open for 9% of the time, Pallas kernels for 0%

commit v1 on v0

--- a/solution.py
+++ b/solution.py
@@ -61,7 +61,7 @@
         partial_value.astype(jnp.bfloat16), "tp", scatter_dimension=1, tiled=True
     ).astype(jnp.float32)
     low_tokens = low_slots.reshape(slots * longest, doubled_rank)[back]
-    low = lax.psum(low_tokens.astype(jnp.bfloat16), "tp").astype(jnp.float32)
+    low = jnp.sum(lax.all_gather(low_tokens.astype(jnp.bfloat16), "tp"), axis=0).astype(jnp.float32)
     half = lax.axis_index("tp") * column_range // half_cols
     low_half = lax.dynamic_slice_in_dim(low, half * rank_rows, rank_rows, 1)
     low_padded = jnp.where(live[:, :, None], low_half[take], jnp.float32(0.0))

time: 313 us -> 313 us (level)
  the two profiles are of different devices: /device:TPU:8 before, /device:TPU:24 now
where the time goes in v1:
time: 313 us; the launch traced here: 312 us
  waiting for transfers between devices  203 us (65%)
  blocking collectives  47.1 us (15%)
  local copies, waits for them, and re-layouts  24.2 us (8%)
  between operations  13.6 us (4%)
  starting transfers between devices  11.7 us (4%)
  matrix products  7.52 us (2%)
  other arithmetic  4.61 us (1%)
    all_to_all x1, waiting for transfers between devices, local(): lax.all_to_all(adapter_down_weight[wanted_rows], 'ad', split_axis=0, conc...  187 us
    all_to_all x1, blocking collectives, local(): lax.all_to_all(slot_ids.reshape(n_ad, OWNER_SLOTS), 'ad', split_axis=0, c...  33 us
    all_to_all x1, waiting for transfers between devices, local(): lax.all_to_all(selected_up_factor, 'ad', split_axis=0, concat_axis=0, til...  16.4 us
    all_gather x1, blocking collectives, local(): lax.all_gather(low_tokens.astype(jnp.bfloat16), 'tp')  14.2 us
  transfers between devices with their start and end apart: 3, of which 2 were waited for; matrix products, arithmetic and copies ran while one was open for 9% of the time, Pallas kernels for 0%

profile of v1, /device:TPU:24, one launch (start us, length us, event | category | flops | bytes accessed | tf_op | source)
XLA Modules:
  0.0 312.2 jit_solution(8895572207374463784)
XLA Ops:
  6.5 0.8 and_select_fusion
  7.4 0.2 convert_reduce_fusion.1
  7.8 33.0 %all_to_all.22 = s32[64,1,2]{2,1,0:T(1,128)S(1)} all-to-all(s32[64,1,2]{2,1,0:T(1,128)S(1)} %bitcast.43), channel_id=1, replica_groups=mesh['tp'=8,'ad'=64] {'ad'}, dimensions={0} | all-to-all | bytes 1024 | tf_op jit(solution)/shard_map/all_to_all | solution.py:43
  41.1 3.7 %gather_fusion.3 = bf16[128,32,512]{2,1,0:T(8,128)(2,1)} fusion(bf16[8,32,512]{2,1,0:T(8,128)(2,1)} %param.8, s32[1024]{0:T(1024)S(1)} %pad_clamp_fusion.2), kind=kCustom, calls=%fused_computation.3 | custom fusion | bytes 8389120 | tf_op jit(solution)/shard_map/gather | solution.py:49
  44.8 5.8 %all-to-all-start.1 = ((bf16[64,2,32,512]{3,2,1,0:T(8,128)(2,1)}), bf16[64,2,32,512]{3,2,1,0:T(8,128)(2,1)}, u32[]{:S(2)}, u32[]{:S(2)}) async-start(bf16[64,2,32,512]{3,2,1,0:T(8,128)(2,1)} %bitcast.40), calls=%async_computation.2 | async-start | bytes 8388608 | tf_op jit(solution)/shard_map/all_to_all | solution.py:48
  50.7 1.7 gather_fusion.8
  52.4 187.1 %all-to-all-done.1 = bf16[64,2,32,512]{3,2,1,0:T(8,128)(2,1)} async-done(((bf16[64,2,32,512]{3,2,1,0:T(8,128)(2,1)}), bf16[64,2,32,512]{3,2,1,0:T(8,128)(2,1)}, u32[]{:S(2)}, u32[]{:S(2)}) %all-to-all-start.1) | async-done | bytes 4194336 | tf_op jit(solution)/shard_map/all_to_all | solution.py:48
  239.4 5.8 %all-to-all-start.2 = ((bf16[64,2,16,256]{3,2,1,0:T(8,128)(2,1)}), bf16[64,2,16,256]{3,2,1,0:T(8,128)(2,1)S(1)}, u32[]{:S(2)}, u32[]{:S(2)}) async-start(bf16[64,2,16,256]{3,2,1,0:T(8,128)(2,1)} %bitcast.17), calls=%async_computation.3 | async-start | bytes 2097152 | tf_op jit(solution)/shard_map/all_to_all | solution.py:51
  245.4 1.7 convolution_convert_fusion
  247.6 1.9 gather_fusion.4
  249.4 1.9 gather_fusion.5
  251.3 1.2 gather_fusion.1
  252.6 1.2 gather_fusion
  254.1 5.1 %gather_fusion.2 = bf16[1024,512]{1,0:T(8,128)(2,1)} fusion(bf16[256,512]{1,0:T(8,128)(2,1)S(1)} %copy-done.2, s32[1024]{0:T(1024)S(1)} %broadcast_clamp_fusion), kind=kCustom, calls=%fused_computation.2 | custom fusion | bytes 2101248 | tf_op jit(solution)/shard_map/gather | solution.py:39
  259.3 3.8 %convolution_bitcast_fusion.1 = bf16[1024,32]{1,0:T(8,128)(2,1)S(1)} fusion(bf16[128,32,512]{2,1,0:T(8,128)(2,1)} %bitcast.8, bf16[1024,512]{1,0:T(8,128)(2,1)} %gather_fusion.2, pred[128,8]{1,0:T(8,128)(4,1)S(1)} %fusion.4), kind=kOutput, calls=%fused_computation.12 | convolution fusion | flops 34078720 | bytes 5309440 | tf_op jit(solution)/shard_map/smd,scd->smc/dot_general | solution.py:53
  263.1 0.9 gather_fusion.6
  264.0 14.2 %all-gather = bf16[2048,32]{1,0:T(8,128)(2,1)} all-gather(bf16[256,32]{1,0:T(8,128)(2,1)S(1)} %gather_fusion.6), channel_id=2, replica_groups=mesh['tp'=8,'ad'=64] {'tp'}, dimensions={0}, use_global_device_ids=true | all-gather | bytes 147456 | tf_op jit(solution)/shard_map/all_gather | solution.py:64
  278.2 1.2 reduce_sum.58
  279.4 4.0 %gather_fusion.7 = f32[1024,16]{1,0:T(8,128)} fusion(f32[256,16]{1,0:T(8,128)S(1)} %dynamic-slice_convert_fusion, s32[1024]{0:T(1024)S(1)} %broadcast_clamp_fusion), kind=kCustom, calls=%fused_computation.7 | custom fusion | bytes 135168 | tf_op jit(solution)/shard_map/gather | solution.py:67
  283.4 16.4 %all-to-all-done.2 = bf16[64,2,16,256]{3,2,1,0:T(8,128)(2,1)S(1)} async-done(((bf16[64,2,16,256]{3,2,1,0:T(8,128)(2,1)}), bf16[64,2,16,256]{3,2,1,0:T(8,128)(2,1)S(1)}, u32[]{:S(2)}, u32[]{:S(2)}) %all-to-all-start.2) | async-done | bytes 1048608 | tf_op jit(solution)/shard_map/all_to_all | solution.py:51
  299.8 1.0 copy-done.4
  300.8 2.0 convolution_bitcast_fusion
  302.8 1.0 gather_fusion.9
  303.8 1.6 add_convert_fusion
  (38 shorter events, 1.6 us)
Async XLA Ops:
  6.5 238.8 %copy-start = (bf16[512,2048]{1,0:T(8,128)(2,1)S(1)}, bf16[512,2048]{1,0:T(8,128)(2,1)}, u32[]{:S(2)}) copy-start(bf16[512,2048]{1,0:T(8,128)(2,1)} %param.7) | copy-start | bytes 6291460
  44.8 5.8 %copy-start.3 = (bf16[8,16,256]{2,1,0:T(8,128)(2,1)S(1)}, bf16[8,16,256]{2,1,0:T(8,128)(2,1)}, u32[]{:S(2)}) copy-start(bf16[8,16,256]{2,1,0:T(8,128)(2,1)} %param.9) | copy-start | bytes 196612
  44.8 194.6 %all-to-all-start.1 = ((bf16[64,2,32,512]{3,2,1,0:T(8,128)(2,1)}), bf16[64,2,32,512]{3,2,1,0:T(8,128)(2,1)}, u32[]{:S(2)}, u32[]{:S(2)}) async-start(bf16[64,2,32,512]{3,2,1,0:T(8,128)(2,1)} %bitcast.40), calls=%async_computation.2 | async-start | bytes 8388608 | tf_op jit(solution)/shard_map/all_to_all | solution.py:48
  50.6 194.7 %copy-start.2 = (bf16[256,512]{1,0:T(8,128)(2,1)S(1)}, bf16[256,512]{1,0:T(8,128)(2,1)}, u32[]{:S(2)}) copy-start(bf16[256,512]{1,0:T(8,128)(2,1)} %param.6) | copy-start | bytes 786436
  50.7 196.5 %copy-start.1 = (s32[1,64]{1,0:T(1,128)S(1)}, s32[1,64]{1,0:T(1,128)}, u32[]{:S(2)}) copy-start(s32[1,64]{1,0:T(1,128)} %param.11) | copy-start | bytes 772
  239.4 60.3 %all-to-all-start.2 = ((bf16[64,2,16,256]{3,2,1,0:T(8,128)(2,1)}), bf16[64,2,16,256]{3,2,1,0:T(8,128)(2,1)S(1)}, u32[]{:S(2)}, u32[]{:S(2)}) async-start(bf16[64,2,16,256]{3,2,1,0:T(8,128)(2,1)} %bitcast.17), calls=%async_computation.3 | async-start | bytes 2097152 | tf_op jit(solution)/shard_map/all_to_all | solution.py:51
  245.3 58.5 %reduce-scatter.2.cloned.1.call-start = ((), (), s32[]{:S(2)}) async-start(), calls=%async_computation.4 | async-start | bytes 1179648 | tf_op jit(solution)/shard_map/reduce_scatter | solution.py:60
  299.8 1.0 copy-start.4
Sparse Core Ops, SparseCore 0:
  249.0 38.0 reduce-scatter.1
